TPU v7x, 128 devices: a whole 4x4x4 slice. The times are simulated.
128 devices in a mesh: dp: 16 (over x_lo, z, core), tensor: 8 (over y, x_hi).
Axes of the slice: x: 4 (x_hi: 2, x_lo: 2; x = x_hi * 2 + x_lo), y: 4, z: 4, core: 2. Of those that a mesh axis runs over, the one named last changes fastest.
Arguments:
- queries: bfloat16 [49152, 1024], P('dp', 'tensor'), may hold values from -80 to 80
- keys: bfloat16 [49152, 128], P('dp'), may hold values from -6 to 6
- values: bfloat16 [49152, 128], P('dp'), may hold values from -6 to 6
- dout: bfloat16 [49152, 1024], P('dp', 'tensor'), may hold values from -6 to 6
- offsets: int32 [8], replicated, may hold values from 0 to 2047
- lengths: int32 [16], P('dp'), may hold values from 256 to 1024
Outputs:
- dq: bfloat16 [49152, 1024], P('dp', 'tensor')
- dk: bfloat16 [49152, 128], P('dp')
- dv: bfloat16 [49152, 128], P('dp')
All inputs are finite; a program needn't handle non-finite values.
Results may differ from a plain program's by a relative error of at most 0.015.
Values may be sent and summed in bfloat16 or wider, within the bound.
A program may use at most 128 MiB of HBM per device.

v0:
```python
import jax
import jax.numpy as jnp
from jax import lax
from jax.sharding import PartitionSpec as P

PH = 2048


def passed_along(value, axis, steps):
    count = lax.axis_size(axis)
    pairs = [(source, (source + steps) % count) for source in range(count)]
    return lax.ppermute(value, axis, pairs)


def block_terms(query, grad_out, positions, key_all, value_all, key_pos, offset):
    scale = 1.0 / query.shape[1] ** 0.5
    scores = (
        lax.dot_general(
            query, key_all, (((1,), (1,)), ((), ())), preferred_element_type=jnp.float32
        )
        * scale
    )
    allowed = (key_pos[None, :] <= positions[:, None]) & (
        (key_pos[None, :] >= offset) | (key_pos[None, :] == positions[:, None])
    )
    scores = jnp.where(allowed, scores, -jnp.inf)
    top = jnp.max(scores, axis=1, keepdims=True)
    expo = jnp.exp(scores - top)
    probs = expo / jnp.sum(expo, axis=1, keepdims=True)
    probs_b = probs.astype(jnp.bfloat16)
    output = jnp.dot(probs_b, value_all, preferred_element_type=jnp.float32)
    delta = jnp.sum(grad_out.astype(jnp.float32) * output, axis=1)
    dprobs = lax.dot_general(
        grad_out, value_all, (((1,), (1,)), ((), ())), preferred_element_type=jnp.float32
    )
    dscores = (probs * (dprobs - delta[:, None]) * scale).astype(jnp.bfloat16)
    grad_q = jnp.dot(dscores, key_all, preferred_element_type=jnp.float32)
    grad_k = lax.dot_general(
        dscores, query, (((0,), (0,)), ((), ())), preferred_element_type=jnp.float32
    )
    grad_v = lax.dot_general(
        probs_b, grad_out, (((0,), (0,)), ((), ())), preferred_element_type=jnp.float32
    )
    return (grad_q, grad_k, grad_v)


def per_device(queries, keys, values, dout, offsets, lengths):
    half = lax.axis_size("dp") // 2
    index = lax.axis_index("dp")
    side = index >= half
    offset = lax.dynamic_index_in_dim(offsets, index % half, 0, keepdims=False)
    length = lengths[0]
    rows = queries.shape[0]
    head_dim = keys.shape[1]
    resp_rows = rows - PH
    mine = jnp.concatenate([keys[:PH], values[:PH]], axis=1)
    partner = passed_along(mine, "dp", half)
    first = jnp.where(side, partner, mine)
    second = jnp.where(side, mine, partner)
    key_all = jnp.concatenate([first[:, :head_dim], second[:, :head_dim], keys[PH:]])
    value_all = jnp.concatenate([first[:, head_dim:], second[:, head_dim:], values[PH:]])
    key_rows = key_all.shape[0]
    positions = jnp.concatenate(
        [
            side.astype(jnp.int32) * PH + jnp.arange(PH, dtype=jnp.int32),
            2 * PH + jnp.arange(resp_rows, dtype=jnp.int32),
        ]
    )
    valid = jnp.concatenate(
        [jnp.ones((PH,), jnp.bool_), jnp.arange(resp_rows, dtype=jnp.int32) < length]
    )
    masked = jnp.where(valid[:, None], dout, jnp.zeros_like(dout))
    key_pos = jnp.arange(key_rows, dtype=jnp.int32)
    block = min(512, rows)
    blocks = rows // block
    grad_k = jnp.zeros((key_rows, head_dim), jnp.float32)
    grad_v = jnp.zeros((key_rows, head_dim), jnp.float32)
    block_pos = positions.reshape(blocks, block)
    head_q = queries.reshape(blocks, block, head_dim)
    head_d = masked.reshape(blocks, block, head_dim)

    def step_block(carry, items):
        gq, gk, gv = block_terms(items[0], items[1], items[2], key_all, value_all, key_pos, offset)
        return ((carry[0] + gk, carry[1] + gv), gq.astype(jnp.bfloat16))

    (grad_k, grad_v), head_grad = lax.scan(
        step_block, (grad_k, grad_v), (head_q, head_d, block_pos)
    )
    grad_qs = head_grad.reshape(rows, head_dim)
    grads = jnp.concatenate([grad_k, grad_v], axis=1)
    own = jnp.where(side, grads[PH : 2 * PH], grads[:PH])
    other = jnp.where(side, grads[:PH], grads[PH : 2 * PH])
    response = grads[2 * PH :]
    received = passed_along(other, "dp", half)
    total = lax.psum(jnp.concatenate([own + received, response]), "tensor")
    finished = total.astype(jnp.bfloat16)
    return (grad_qs, finished[:, :head_dim], finished[:, head_dim:])


def solution(mesh):
    return jax.shard_map(
        per_device,
        mesh=mesh,
        in_specs=(P("dp", "tensor"), P("dp", None), P("dp", None), P("dp", "tensor"), P(), P("dp")),
        out_specs=(P("dp", "tensor"), P("dp", None), P("dp", None)),
        check_vma=False,
    )
```

profile of v0, /device:TPU:0, one launch (start us, length us, event | category | flops | bytes accessed | tf_op | source)
XLA Modules:
  0.0 469.1 jit_solution(9047942482505593521)
XLA Ops:
  10.9 18.9 %collective-permute-done = bf16[2048,256]{1,0:T(8,128)(2,1)} collective-permute-done((bf16[2048,256]{1,0:T(8,128)(2,1)}, bf16[2048,256]{1,0:T(8,128)(2,1)}, u32[]{:S(2)}, u32[]{:S(2)}) %collective-permute-start) | collective-permute-done | bytes 1048608 | tf_op jit(solution)/shard_map/ppermute | solution.py:12
  34.7 252.9 %while.16 = (s32[]{:T(128)}, f32[5120,128]{1,0:T(8,128)}, f32[5120,128]{1,0:T(8,128)S(1)}, bf16[6,512,128]{2,1,0:T(8,128)(2,1)}, s32[6,512]{1,0:T(8,128)S(1)}, /...) while((s32[]{:T(128)}, f32[5120,128]{1,0:T(8,128)}, ...), condition=%wide.region_4.5_spmd.clone.clone, body=%wide.region_0.4_spmd.clone.clone.sunk | while | flops 4073983488 | bytes 179601168 | solution.py:86
  49.8 6.3 %fusion.65 = f32[512]{0:T(512)S(1)} fusion(bf16[5120,128]{1,0:T(8,128)(2,1)} %get-tuple-element.273, f32[512,5120]{1,0:T(8,128)} %fusion.64, bf16[1,512,128]{1,2,0:T(8,128)(2,1)S(1)} %copy.12), kind=kOutput, calls=%fused_computation.17.clone.1 | convolution fusion | flops 673906176 | bytes 11929600 | tf_op jit(solution)/shard_map/while/body/eval_jaxpr/dot_general | solution.py:31
  69.2 6.9 %convolution_add_fusion.5 = f32[5120,128]{1,0:T(8,128)S(1)} fusion(f32[5120,128]{1,0:T(8,128)S(1)} %get-tuple-element.254, f32[512,5120]{1,0:T(8,128)} %fusion.64, pred[]{:T(512)S(6)} %compare.5, bf16[1,512,128]{2,1,0:T(8,128)(2,1)S(1)} %constant_dynamic-slice_fusion.5), kind=kOutput, calls=%fused_computation.10.clone.1 | convolution fusion | flops 675020800 | bytes 15859713 | tf_op jit(solution)/shard_map/while/body/eval_jaxpr/dot_general | solution.py:41
  76.8 6.0 %fusion.62 = (f32[512]{0:T(512)S(1)}, f32[512,5120]{1,0:T(8,128)S(1)}) fusion(bf16[5120,128]{1,0:T(8,128)(2,1)} %get-tuple-element.271, bf16[6,512,128]{2,1,0:T(8,128)(2,1)} %get-tuple-element.270, s32[]{:T(128)} %get-tuple-element.252, pred[5120]{0:T(1024)(128)(4,1)S(1)} %iota_compare_fusion.5, s32[512]{0:T(512)S(1)} %bitcast.59), kind=kOutput, calls=%fused_computation.46.clone.1 | convolution fusion | flops 689438208 | bytes 11937280 | tf_op jit(solution)/shard_map/while/body/eval_jaxpr/dot_general | solution.py:18
  91.3 6.3 %fusion.65 = f32[512]{0:T(512)S(1)} fusion(bf16[5120,128]{1,0:T(8,128)(2,1)} %get-tuple-element.273, f32[512,5120]{1,0:T(8,128)} %fusion.64, bf16[1,512,128]{1,2,0:T(8,128)(2,1)S(1)} %copy.12), kind=kOutput, calls=%fused_computation.17.clone.1 | convolution fusion | flops 673906176 | bytes 11929600 | tf_op jit(solution)/shard_map/while/body/eval_jaxpr/dot_general | solution.py:31
  102.8 6.5 %convolution_add_fusion.4 = f32[5120,128]{1,0:T(8,128)} fusion(bf16[512,5120]{1,0:T(8,128)(2,1)} %multiply_convert_fusion.2, f32[5120,128]{1,0:T(8,128)} %get-tuple-element.253, pred[]{:T(512)S(6)} %compare.5, bf16[6,512,128]{2,1,0:T(8,128)(2,1)} %get-tuple-element.270, s32[]{:T(128)} %get-tuple-element.252), kind=kOutput, calls=%fused_computation.11.clone.1 | convolution fusion | flops 672399360 | bytes 10617345 | tf_op jit(solution)/shard_map/while/body/eval_jaxpr/dot_general | solution.py:38
  111.5 6.9 %convolution_add_fusion.5 = f32[5120,128]{1,0:T(8,128)S(1)} fusion(f32[5120,128]{1,0:T(8,128)S(1)} %get-tuple-element.254, f32[512,5120]{1,0:T(8,128)} %fusion.64, pred[]{:T(512)S(6)} %compare.5, bf16[1,512,128]{2,1,0:T(8,128)(2,1)S(1)} %constant_dynamic-slice_fusion.5), kind=kOutput, calls=%fused_computation.10.clone.1 | convolution fusion | flops 675020800 | bytes 15859713 | tf_op jit(solution)/shard_map/while/body/eval_jaxpr/dot_general | solution.py:41
  119.1 6.0 %fusion.62 = (f32[512]{0:T(512)S(1)}, f32[512,5120]{1,0:T(8,128)S(1)}) fusion(bf16[5120,128]{1,0:T(8,128)(2,1)} %get-tuple-element.271, bf16[6,512,128]{2,1,0:T(8,128)(2,1)} %get-tuple-element.270, s32[]{:T(128)} %get-tuple-element.252, pred[5120]{0:T(1024)(128)(4,1)S(1)} %iota_compare_fusion.5, s32[512]{0:T(512)S(1)} %bitcast.59), kind=kOutput, calls=%fused_computation.46.clone.1 | convolution fusion | flops 689438208 | bytes 11937280 | tf_op jit(solution)/shard_map/while/body/eval_jaxpr/dot_general | solution.py:18
  133.6 6.3 %fusion.65 = f32[512]{0:T(512)S(1)} fusion(bf16[5120,128]{1,0:T(8,128)(2,1)} %get-tuple-element.273, f32[512,5120]{1,0:T(8,128)} %fusion.64, bf16[1,512,128]{1,2,0:T(8,128)(2,1)S(1)} %copy.12), kind=kOutput, calls=%fused_computation.17.clone.1 | convolution fusion | flops 673906176 | bytes 11929600 | tf_op jit(solution)/shard_map/while/body/eval_jaxpr/dot_general | solution.py:31
  145.1 6.5 %convolution_add_fusion.4 = f32[5120,128]{1,0:T(8,128)} fusion(bf16[512,5120]{1,0:T(8,128)(2,1)} %multiply_convert_fusion.2, f32[5120,128]{1,0:T(8,128)} %get-tuple-element.253, pred[]{:T(512)S(6)} %compare.5, bf16[6,512,128]{2,1,0:T(8,128)(2,1)} %get-tuple-element.270, s32[]{:T(128)} %get-tuple-element.252), kind=kOutput, calls=%fused_computation.11.clone.1 | convolution fusion | flops 672399360 | bytes 10617345 | tf_op jit(solution)/shard_map/while/body/eval_jaxpr/dot_general | solution.py:38
  153.8 6.9 %convolution_add_fusion.5 = f32[5120,128]{1,0:T(8,128)S(1)} fusion(f32[5120,128]{1,0:T(8,128)S(1)} %get-tuple-element.254, f32[512,5120]{1,0:T(8,128)} %fusion.64, pred[]{:T(512)S(6)} %compare.5, bf16[1,512,128]{2,1,0:T(8,128)(2,1)S(1)} %constant_dynamic-slice_fusion.5), kind=kOutput, calls=%fused_computation.10.clone.1 | convolution fusion | flops 675020800 | bytes 15859713 | tf_op jit(solution)/shard_map/while/body/eval_jaxpr/dot_general | solution.py:41
  175.9 6.3 %fusion.65 = f32[512]{0:T(512)S(1)} fusion(bf16[5120,128]{1,0:T(8,128)(2,1)} %get-tuple-element.273, f32[512,5120]{1,0:T(8,128)} %fusion.64, bf16[1,512,128]{1,2,0:T(8,128)(2,1)S(1)} %copy.12), kind=kOutput, calls=%fused_computation.17.clone.1 | convolution fusion | flops 673906176 | bytes 11929600 | tf_op jit(solution)/shard_map/while/body/eval_jaxpr/dot_general | solution.py:31
  187.4 6.5 %convolution_add_fusion.4 = f32[5120,128]{1,0:T(8,128)} fusion(bf16[512,5120]{1,0:T(8,128)(2,1)} %multiply_convert_fusion.2, f32[5120,128]{1,0:T(8,128)} %get-tuple-element.253, pred[]{:T(512)S(6)} %compare.5, bf16[6,512,128]{2,1,0:T(8,128)(2,1)} %get-tuple-element.270, s32[]{:T(128)} %get-tuple-element.252), kind=kOutput, calls=%fused_computation.11.clone.1 | convolution fusion | flops 672399360 | bytes 10617345 | tf_op jit(solution)/shard_map/while/body/eval_jaxpr/dot_general | solution.py:38
  196.1 6.9 %convolution_add_fusion.5 = f32[5120,128]{1,0:T(8,128)S(1)} fusion(f32[5120,128]{1,0:T(8,128)S(1)} %get-tuple-element.254, f32[512,5120]{1,0:T(8,128)} %fusion.64, pred[]{:T(512)S(6)} %compare.5, bf16[1,512,128]{2,1,0:T(8,128)(2,1)S(1)} %constant_dynamic-slice_fusion.5), kind=kOutput, calls=%fused_computation.10.clone.1 | convolution fusion | flops 675020800 | bytes 15859713 | tf_op jit(solution)/shard_map/while/body/eval_jaxpr/dot_general | solution.py:41
  203.7 6.0 %fusion.62 = (f32[512]{0:T(512)S(1)}, f32[512,5120]{1,0:T(8,128)S(1)}) fusion(bf16[5120,128]{1,0:T(8,128)(2,1)} %get-tuple-element.271, bf16[6,512,128]{2,1,0:T(8,128)(2,1)} %get-tuple-element.270, s32[]{:T(128)} %get-tuple-element.252, pred[5120]{0:T(1024)(128)(4,1)S(1)} %iota_compare_fusion.5, s32[512]{0:T(512)S(1)} %bitcast.59), kind=kOutput, calls=%fused_computation.46.clone.1 | convolution fusion | flops 689438208 | bytes 11937280 | tf_op jit(solution)/shard_map/while/body/eval_jaxpr/dot_general | solution.py:18
  218.2 6.3 %fusion.65 = f32[512]{0:T(512)S(1)} fusion(bf16[5120,128]{1,0:T(8,128)(2,1)} %get-tuple-element.273, f32[512,5120]{1,0:T(8,128)} %fusion.64, bf16[1,512,128]{1,2,0:T(8,128)(2,1)S(1)} %copy.12), kind=kOutput, calls=%fused_computation.17.clone.1 | convolution fusion | flops 673906176 | bytes 11929600 | tf_op jit(solution)/shard_map/while/body/eval_jaxpr/dot_general | solution.py:31
  229.7 6.5 %convolution_add_fusion.4 = f32[5120,128]{1,0:T(8,128)} fusion(bf16[512,5120]{1,0:T(8,128)(2,1)} %multiply_convert_fusion.2, f32[5120,128]{1,0:T(8,128)} %get-tuple-element.253, pred[]{:T(512)S(6)} %compare.5, bf16[6,512,128]{2,1,0:T(8,128)(2,1)} %get-tuple-element.270, s32[]{:T(128)} %get-tuple-element.252), kind=kOutput, calls=%fused_computation.11.clone.1 | convolution fusion | flops 672399360 | bytes 10617345 | tf_op jit(solution)/shard_map/while/body/eval_jaxpr/dot_general | solution.py:38
  238.4 6.9 %convolution_add_fusion.5 = f32[5120,128]{1,0:T(8,128)S(1)} fusion(f32[5120,128]{1,0:T(8,128)S(1)} %get-tuple-element.254, f32[512,5120]{1,0:T(8,128)} %fusion.64, pred[]{:T(512)S(6)} %compare.5, bf16[1,512,128]{2,1,0:T(8,128)(2,1)S(1)} %constant_dynamic-slice_fusion.5), kind=kOutput, calls=%fused_computation.10.clone.1 | convolution fusion | flops 675020800 | bytes 15859713 | tf_op jit(solution)/shard_map/while/body/eval_jaxpr/dot_general | solution.py:41
  260.4 6.3 %fusion.65 = f32[512]{0:T(512)S(1)} fusion(bf16[5120,128]{1,0:T(8,128)(2,1)} %get-tuple-element.273, f32[512,5120]{1,0:T(8,128)} %fusion.64, bf16[1,512,128]{1,2,0:T(8,128)(2,1)S(1)} %copy.12), kind=kOutput, calls=%fused_computation.17.clone.1 | convolution fusion | flops 673906176 | bytes 11929600 | tf_op jit(solution)/shard_map/while/body/eval_jaxpr/dot_general | solution.py:31
  272.0 6.5 %convolution_add_fusion.4 = f32[5120,128]{1,0:T(8,128)} fusion(bf16[512,5120]{1,0:T(8,128)(2,1)} %multiply_convert_fusion.2, f32[5120,128]{1,0:T(8,128)} %get-tuple-element.253, pred[]{:T(512)S(6)} %compare.5, bf16[6,512,128]{2,1,0:T(8,128)(2,1)} %get-tuple-element.270, s32[]{:T(128)} %get-tuple-element.252), kind=kOutput, calls=%fused_computation.11.clone.1 | convolution fusion | flops 672399360 | bytes 10617345 | tf_op jit(solution)/shard_map/while/body/eval_jaxpr/dot_general | solution.py:38
  280.7 6.9 %convolution_add_fusion.5 = f32[5120,128]{1,0:T(8,128)S(1)} fusion(f32[5120,128]{1,0:T(8,128)S(1)} %get-tuple-element.254, f32[512,5120]{1,0:T(8,128)} %fusion.64, pred[]{:T(512)S(6)} %compare.5, bf16[1,512,128]{2,1,0:T(8,128)(2,1)S(1)} %constant_dynamic-slice_fusion.5), kind=kOutput, calls=%fused_computation.10.clone.1 | convolution fusion | flops 675020800 | bytes 15859713 | tf_op jit(solution)/shard_map/while/body/eval_jaxpr/dot_general | solution.py:41
  292.0 44.7 %collective-permute-done.1 = f32[2048,256]{1,0:T(8,128)S(1)} collective-permute-done((f32[2048,256]{1,0:T(8,128)S(1)}, f32[2048,256]{1,0:T(8,128)S(1)}, u32[]{:S(2)}, u32[]{:S(2)}) %collective-permute-start.1) | collective-permute-done | bytes 2097184 | tf_op jit(solution)/shard_map/ppermute | solution.py:12
  337.3 129.2 %all-reduce.2 = bf16[3072,256]{1,0:T(8,128)(2,1)} all-reduce(f32[3072,256]{1,0:T(8,128)S(1)} %pad_maximum_fusion), channel_id=1, replica_groups=mesh['dp'=16,'tensor'=8] {'tensor'}, use_global_device_ids=true, to_apply=%region_5.6 | all-reduce | flops 786432 | bytes 4718592 | tf_op jit(solution)/shard_map/psum | solution.py:95
  (135 shorter events, 144.3 us)
Async XLA Ops:
  4.7 25.0 %collective-permute-start = (bf16[2048,256]{1,0:T(8,128)(2,1)}, bf16[2048,256]{1,0:T(8,128)(2,1)}, u32[]{:S(2)}, u32[]{:S(2)}) collective-permute-start(bf16[2048,256]{1,0:T(8,128)(2,1)} %pad_maximum_fusion.3), channel_id=1, source_target_pairs={{0,64},{8,72},{16,80},{24,88},{32,96},{40,104},{48,112},{56,120},{... | collective-permute-start | bytes 3145736 | tf_op jit(solution)/shard_map/ppermute | solution.py:12
  49.8 7.3 %copy-start = (f32[512,5120]{1,0:T(8,128)S(1)}, f32[512,5120]{1,0:T(8,128)}, u32[]{:S(2)}) copy-start(f32[512,5120]{1,0:T(8,128)} %fusion.64) | copy-start | bytes 31457284 | tf_op jit(solution)/shard_map/while
  49.8 7.6 %copy-start.2 = (bf16[5120,128]{1,0:T(8,128)(2,1)S(1)}, bf16[5120,128]{1,0:T(8,128)(2,1)}, u32[]{:S(2)}) copy-start(bf16[5120,128]{1,0:T(8,128)(2,1)} %get-tuple-element.273) | copy-start | bytes 3932164 | tf_op jit(solution)/shard_map/while
  91.3 7.3 %copy-start = (f32[512,5120]{1,0:T(8,128)S(1)}, f32[512,5120]{1,0:T(8,128)}, u32[]{:S(2)}) copy-start(f32[512,5120]{1,0:T(8,128)} %fusion.64) | copy-start | bytes 31457284 | tf_op jit(solution)/shard_map/while
  91.3 7.6 %copy-start.2 = (bf16[5120,128]{1,0:T(8,128)(2,1)S(1)}, bf16[5120,128]{1,0:T(8,128)(2,1)}, u32[]{:S(2)}) copy-start(bf16[5120,128]{1,0:T(8,128)(2,1)} %get-tuple-element.273) | copy-start | bytes 3932164 | tf_op jit(solution)/shard_map/while
  102.8 6.5 %copy-start.1 = (bf16[512,5120]{1,0:T(8,128)(2,1)S(1)}, bf16[512,5120]{1,0:T(8,128)(2,1)}, u32[]{:S(2)}) copy-start(bf16[512,5120]{1,0:T(8,128)(2,1)} %multiply_convert_fusion.2) | copy-start | bytes 15728644 | tf_op jit(solution)/shard_map/while
  102.8 6.5 %copy-start.4 = (bf16[5120,128]{1,0:T(8,128)(2,1)S(1)}, bf16[5120,128]{1,0:T(8,128)(2,1)}, u32[]{:S(2)}) copy-start(bf16[5120,128]{1,0:T(8,128)(2,1)} %get-tuple-element.271) | copy-start | bytes 3932164 | tf_op jit(solution)/shard_map/while
  133.6 7.3 %copy-start = (f32[512,5120]{1,0:T(8,128)S(1)}, f32[512,5120]{1,0:T(8,128)}, u32[]{:S(2)}) copy-start(f32[512,5120]{1,0:T(8,128)} %fusion.64) | copy-start | bytes 31457284 | tf_op jit(solution)/shard_map/while
  133.6 7.6 %copy-start.2 = (bf16[5120,128]{1,0:T(8,128)(2,1)S(1)}, bf16[5120,128]{1,0:T(8,128)(2,1)}, u32[]{:S(2)}) copy-start(bf16[5120,128]{1,0:T(8,128)(2,1)} %get-tuple-element.273) | copy-start | bytes 3932164 | tf_op jit(solution)/shard_map/while
  145.1 6.5 %copy-start.1 = (bf16[512,5120]{1,0:T(8,128)(2,1)S(1)}, bf16[512,5120]{1,0:T(8,128)(2,1)}, u32[]{:S(2)}) copy-start(bf16[512,5120]{1,0:T(8,128)(2,1)} %multiply_convert_fusion.2) | copy-start | bytes 15728644 | tf_op jit(solution)/shard_map/while
  145.1 6.5 %copy-start.4 = (bf16[5120,128]{1,0:T(8,128)(2,1)S(1)}, bf16[5120,128]{1,0:T(8,128)(2,1)}, u32[]{:S(2)}) copy-start(bf16[5120,128]{1,0:T(8,128)(2,1)} %get-tuple-element.271) | copy-start | bytes 3932164 | tf_op jit(solution)/shard_map/while
  175.8 7.3 %copy-start = (f32[512,5120]{1,0:T(8,128)S(1)}, f32[512,5120]{1,0:T(8,128)}, u32[]{:S(2)}) copy-start(f32[512,5120]{1,0:T(8,128)} %fusion.64) | copy-start | bytes 31457284 | tf_op jit(solution)/shard_map/while
  175.9 7.6 %copy-start.2 = (bf16[5120,128]{1,0:T(8,128)(2,1)S(1)}, bf16[5120,128]{1,0:T(8,128)(2,1)}, u32[]{:S(2)}) copy-start(bf16[5120,128]{1,0:T(8,128)(2,1)} %get-tuple-element.273) | copy-start | bytes 3932164 | tf_op jit(solution)/shard_map/while
  187.4 6.5 %copy-start.1 = (bf16[512,5120]{1,0:T(8,128)(2,1)S(1)}, bf16[512,5120]{1,0:T(8,128)(2,1)}, u32[]{:S(2)}) copy-start(bf16[512,5120]{1,0:T(8,128)(2,1)} %multiply_convert_fusion.2) | copy-start | bytes 15728644 | tf_op jit(solution)/shard_map/while
  187.4 6.5 %copy-start.4 = (bf16[5120,128]{1,0:T(8,128)(2,1)S(1)}, bf16[5120,128]{1,0:T(8,128)(2,1)}, u32[]{:S(2)}) copy-start(bf16[5120,128]{1,0:T(8,128)(2,1)} %get-tuple-element.271) | copy-start | bytes 3932164 | tf_op jit(solution)/shard_map/while
  218.1 7.3 %copy-start = (f32[512,5120]{1,0:T(8,128)S(1)}, f32[512,5120]{1,0:T(8,128)}, u32[]{:S(2)}) copy-start(f32[512,5120]{1,0:T(8,128)} %fusion.64) | copy-start | bytes 31457284 | tf_op jit(solution)/shard_map/while
  218.1 7.6 %copy-start.2 = (bf16[5120,128]{1,0:T(8,128)(2,1)S(1)}, bf16[5120,128]{1,0:T(8,128)(2,1)}, u32[]{:S(2)}) copy-start(bf16[5120,128]{1,0:T(8,128)(2,1)} %get-tuple-element.273) | copy-start | bytes 3932164 | tf_op jit(solution)/shard_map/while
  229.7 6.5 %copy-start.1 = (bf16[512,5120]{1,0:T(8,128)(2,1)S(1)}, bf16[512,5120]{1,0:T(8,128)(2,1)}, u32[]{:S(2)}) copy-start(bf16[512,5120]{1,0:T(8,128)(2,1)} %multiply_convert_fusion.2) | copy-start | bytes 15728644 | tf_op jit(solution)/shard_map/while
  229.7 6.5 %copy-start.4 = (bf16[5120,128]{1,0:T(8,128)(2,1)S(1)}, bf16[5120,128]{1,0:T(8,128)(2,1)}, u32[]{:S(2)}) copy-start(bf16[5120,128]{1,0:T(8,128)(2,1)} %get-tuple-element.271) | copy-start | bytes 3932164 | tf_op jit(solution)/shard_map/while
  260.4 7.3 %copy-start = (f32[512,5120]{1,0:T(8,128)S(1)}, f32[512,5120]{1,0:T(8,128)}, u32[]{:S(2)}) copy-start(f32[512,5120]{1,0:T(8,128)} %fusion.64) | copy-start | bytes 31457284 | tf_op jit(solution)/shard_map/while
  260.4 7.6 %copy-start.2 = (bf16[5120,128]{1,0:T(8,128)(2,1)S(1)}, bf16[5120,128]{1,0:T(8,128)(2,1)}, u32[]{:S(2)}) copy-start(bf16[5120,128]{1,0:T(8,128)(2,1)} %get-tuple-element.273) | copy-start | bytes 3932164 | tf_op jit(solution)/shard_map/while
  272.0 6.5 %copy-start.1 = (bf16[512,5120]{1,0:T(8,128)(2,1)S(1)}, bf16[512,5120]{1,0:T(8,128)(2,1)}, u32[]{:S(2)}) copy-start(bf16[512,5120]{1,0:T(8,128)(2,1)} %multiply_convert_fusion.2) | copy-start | bytes 15728644 | tf_op jit(solution)/shard_map/while
  272.0 6.5 %copy-start.4 = (bf16[5120,128]{1,0:T(8,128)(2,1)S(1)}, bf16[5120,128]{1,0:T(8,128)(2,1)}, u32[]{:S(2)}) copy-start(bf16[5120,128]{1,0:T(8,128)(2,1)} %get-tuple-element.271) | copy-start | bytes 3932164 | tf_op jit(solution)/shard_map/while
  290.1 46.6 %collective-permute-start.1 = (f32[2048,256]{1,0:T(8,128)S(1)}, f32[2048,256]{1,0:T(8,128)S(1)}, u32[]{:S(2)}, u32[]{:S(2)}) collective-permute-start(f32[2048,256]{1,0:T(8,128)S(1)} %slice_select_fusion), channel_id=1, source_target_pairs={{0,64},{8,72},{16,80},{24,88},{32,96},{40,104},{48,112},{56,120},{... | collective-permute-start | bytes 6291464 | tf_op jit(solution)/shard_map/ppermute | solution.py:12
  (6 other events, 21.5 us)
where the time goes:
time: 470 us; the launch traced here: 469 us
  matrix products  190 us (40%)
  blocking collectives  129 us (27%)
  waiting for transfers between devices  63.5 us (14%)
  other arithmetic  57.3 us (12%)
  local copies, waits for them, and re-layouts  23.5 us (5%)
    psum x1, blocking collectives, per_device(): total = lax.psum(jnp.concatenate([own + received, response]), 'tensor')  129 us
    ppermute x2, waiting for transfers between devices, passed_along(): return lax.ppermute(value, axis, pairs)  63.5 us
    dot_general x6, matrix products, block_terms(): lax.dot_general(probs_b, grad_out, (((0,), (0,)), ((), ())), preferred_el...  41.6 us
    dot_general x6, matrix products, block_terms(): lax.dot_general(dscores, query, (((0,), (0,)), ((), ())), preferred_eleme...  38.3 us
    dot_general x6, matrix products, block_terms(): output = jnp.dot(probs_b, value_all, preferred_element_type=jnp.float32)  37.9 us
    dot_general x6, matrix products, block_terms(): lax.dot_general(query, key_all, (((1,), (1,)), ((), ())), preferred_eleme...  36.2 us
    div x6, other arithmetic, block_terms(): probs = expo / jnp.sum(expo, axis=1, keepdims=True)  34.8 us
    dot_general x6, matrix products, block_terms(): lax.dot_general(grad_out, value_all, (((1,), (1,)), ((), ())), preferred_...  23.4 us
  transfers between devices with their start and end apart: 2, of which 2 were waited for; matrix products, arithmetic and copies ran while one was open for 1% of the time, Pallas kernels for 0%

commit v1 on v0

v1 whole, which is shorter than its diff:
```python
import functools

import jax
import jax.numpy as jnp
from jax import lax
from jax.experimental import pallas as pl
from jax.experimental.pallas import tpu as pltpu
from jax.sharding import PartitionSpec as P

MESH = pl.DeviceIdType.MESH
f32 = jnp.float32
bf = jnp.bfloat16

PH = 2048
R = 1024
DH = 128
KEYS = 2 * PH + R
BQ, BK = 256, 512
RG = 64
NT = 8
SLP = PH // NT
SLR = R // NT
NEG = -1e30
SCALE = 1.0 / DH**0.5
CC = SCALE * 1.4426950408889634


def dot_nt(a, b):
    return lax.dot_general(a, b, (((1,), (1,)), ((), ())), preferred_element_type=f32)


def dot_nn(a, b):
    return jnp.dot(a, b, preferred_element_type=f32)


def kernel(
    offs, lens, q, kin, vin, do, dq, dk, dv,
    k, v, dkT, dvT, S0, S1, DP0, DP1, E, P0, P1, D0, D1, mx, mb, la, ta, dqa, dom, qT, dT, bias,
    sendP, sendR, recvP, recvR,
    kv_s, kv_r, p_s, p_r, r_s, r_r, g_s, g_r,
):
    d = lax.axis_index("dp")
    t = lax.axis_index("tensor")
    half = lax.axis_size("dp") // 2
    side = lax.div(d, half)
    pair = lax.rem(d, half)
    offset = offs[pair]
    length = lens[0]

    def peer(b, a):
        return (lax.rem(side + b, 2) * half + pair, lax.rem(t + a, NT))

    barrier = pltpu.get_barrier_semaphore()
    for i in range(1, 2 * NT):
        pl.semaphore_signal(barrier, inc=1, device_id=peer(i // NT, i % NT), device_id_type=MESH)
    pl.semaphore_wait(barrier, 2 * NT - 1)

    flip = t + 1 - 2 * lax.rem(t, 2)
    hp = PH // 2
    kv = []
    for h in range(2):
        dst = (lax.rem(side + 1, 2) * half + pair, t if h == 0 else flip)
        for i, (src, to) in enumerate(((kin, k), (vin, v))):
            rows = pl.ds(pl.multiple_of(side * PH + h * hp, hp), hp)
            c = pltpu.make_async_remote_copy(
                src_ref=src.at[pl.ds(h * hp, hp)], dst_ref=to.at[rows],
                send_sem=kv_s.at[2 * h + i], recv_sem=kv_r.at[2 * h + i],
                device_id=dst, device_id_type=MESH,
            )
            c.start()
            kv.append(c)

    own = pl.ds(pl.multiple_of(side * PH, PH), PH)
    k[own, :] = kin[:PH, :]
    v[own, :] = vin[:PH, :]
    k[2 * PH :, :] = kin[PH:, :]
    v[2 * PH :, :] = vin[PH:, :]
    dom[:PH, :] = do[:PH, :]
    rr = lax.broadcasted_iota(jnp.int32, (R, DH), 0)
    dom[PH:, :] = jnp.where(rr < length, do[PH:, :], jnp.zeros((R, DH), bf))
    kp = lax.broadcasted_iota(jnp.int32, (8, KEYS), 1)
    bias[...] = jnp.where(kp >= offset, 0.0, NEG).astype(f32)
    dkT[...] = jnp.zeros_like(dkT)
    dvT[...] = jnp.zeros_like(dvT)
    for c in kv:
        c.wait_recv()

    NR, NP = R // BQ, PH // BQ
    NB = NR + NP
    T = BK // 128
    SS, DPS, PS, DS = (S0, S1), (DP0, DP1), (P0, P1), (D0, D1)

    def info(j):
        row0 = jnp.where(j < NR, PH + j * BQ, (NP - 1 - (j - NR)) * BQ)
        pos0 = jnp.where(j < NR, 2 * PH + j * BQ, side * PH + row0)
        return pl.multiple_of(row0, BQ), pos0, lax.div(pos0 + BQ - 1, BK) + 1

    def ks(c):
        return pl.ds(pl.multiple_of(c * BK, BK), BK)

    def kt(c, i):
        return pl.ds(pl.multiple_of(c * BK + i * 128, 128), 128)

    def scores(slot, row0, pos0, c, masked):
        S, DP = SS[slot], DPS[slot]
        s = dot_nt(q[pl.ds(row0, BQ), :], k[ks(c), :])
        if masked:
            cols = lax.broadcasted_iota(jnp.int32, (RG, 128), 1)
        for r in range(0, BQ, RG):
            m = mx[r : r + RG, :]
            for i in range(T):
                st = s[r : r + RG, i * 128 : (i + 1) * 128]
                if masked:
                    rows = lax.broadcasted_iota(jnp.int32, (RG, 128), 0) + (pos0 - c * BK + r)
                    ct = cols + i * 128
                    ok = (ct < rows) & (ct + c * BK >= offset) | (ct == rows)
                    st = jnp.where(ok, st, NEG)
                else:
                    st = st + bias[0:1, kt(c, i)]
                S[r : r + RG, kt(c, i)] = st
                m = jnp.maximum(m, st)
            mx[r : r + RG, :] = m
        DP[:, ks(c)] = dot_nt(dom[pl.ds(row0, BQ), :], v[ks(c), :])

    def row_max():
        mb[...] = jnp.broadcast_to(jnp.max(mx[...], axis=1, keepdims=True) * CC, (BQ, 128))
        mx[...] = jnp.full((BQ, 128), NEG, f32)

    def expo(slot, c):
        S, DP = SS[slot], DPS[slot]
        for r in range(0, BQ, RG):
            l, tt, m = la[r : r + RG, :], ta[r : r + RG, :], mb[r : r + RG, :]
            for i in range(T):
                e = jnp.exp2(S[r : r + RG, kt(c, i)] * CC - m)
                l = l + e
                tt = tt + e * DP[r : r + RG, kt(c, i)]
                E[r : r + RG, kt(c, i)] = e
            la[r : r + RG, :] = l
            ta[r : r + RG, :] = tt

    def grads_in(slot, h, c2):
        DP, Pb, Db = DPS[slot], PS[h], DS[h]
        for r in range(0, BQ, RG):
            rl, dl = la[r : r + RG, :], ta[r : r + RG, :]
            for i in range(2):
                sl = pl.ds(pl.multiple_of(c2 * 256 + i * 128, 128), 128)
                p = E[r : r + RG, sl] * rl
                x = p * (DP[r : r + RG, sl] - dl)
                Pb[r : r + RG, i * 128 : (i + 1) * 128] = p.astype(bf)
                Db[r : r + RG, i * 128 : (i + 1) * 128] = x.astype(bf)

    def grads_out(h, c2):
        Pb, Db = PS[h], DS[h]
        sl = pl.ds(pl.multiple_of(c2 * 256, 256), 256)
        dvT[:, sl] += dot_nn(dT[...], Pb[...])
        dkT[:, sl] += dot_nn(qT[...], Db[...])
        dqa[...] += dot_nn(Db[...], k[sl, :])

    def loop(lo, hi, f):
        def body(c, _):
            f(c)
            return 0

        lax.fori_loop(lo, hi, body, 0)

    def prompt_copy(b, a):
        ts = lax.rem(t + a, NT)
        ss = lax.rem(side + b, 2)
        return pltpu.make_async_remote_copy(
            src_ref=sendP.at[ss * NT + ts], dst_ref=recvP.at[b * NT + a],
            send_sem=p_s.at[b * NT + a], recv_sem=p_r.at[b * NT + a],
            device_id=peer(b, a), device_id_type=MESH,
        )

    def resp_copy(a):
        ts = lax.rem(t + a, NT)
        return pltpu.make_async_remote_copy(
            src_ref=sendR.at[ts], dst_ref=recvR.at[a],
            send_sem=r_s.at[a], recv_sem=r_r.at[a],
            device_id=peer(0, a), device_id_type=MESH,
        )

    def pack_prompt(i):
        sl = pl.ds(pl.multiple_of(i * SLP, SLP), SLP)
        sendP[i, :DH, :] = (dkT[:, sl] * SCALE).astype(bf)
        sendP[i, DH:, :] = dvT[:, sl].astype(bf)

    def send_other():
        loop(0, NT, lambda i: pack_prompt(lax.rem(side + 1, 2) * NT + i))
        for a in range(NT):
            prompt_copy(1, a).start()

    def send_resp():
        for i in range(NT):
            sl = slice(2 * PH + i * SLR, 2 * PH + (i + 1) * SLR)
            sendR[i, :DH, :] = (dkT[:, sl] * SCALE).astype(bf)
            sendR[i, DH:, :] = dvT[:, sl].astype(bf)
        for a in range(1, NT):
            resp_copy(a).start()

    mx[...] = jnp.full((BQ, 128), NEG, f32)
    row0, pos0, n0 = info(jnp.int32(0))
    loop(0, n0 - 1, lambda c: scores(0, row0, pos0, c, False))
    scores(0, row0, pos0, n0 - 1, True)
    row_max()

    def block(j, slot):
        nxt = 1 - slot
        row0, _, n = info(j)
        row1, pos1, n1 = info(j + 1)
        la[...] = jnp.zeros((BQ, 128), f32)
        ta[...] = jnp.zeros((BQ, 128), f32)
        last = j == NB - 1
        na = jnp.where(last, 0, n1 - 1)
        m = jnp.minimum(na, n)

        def both(c):
            expo(slot, c)
            scores(nxt, row1, pos1, c, False)

        loop(0, m, both)
        loop(m, na, lambda c: scores(nxt, row1, pos1, c, False))
        loop(m, n, lambda c: expo(slot, c))
        rl = 1.0 / jnp.sum(la[...], axis=1, keepdims=True)
        dl = jnp.sum(ta[...], axis=1, keepdims=True) * rl
        la[...] = jnp.broadcast_to(rl, (BQ, 128))
        ta[...] = jnp.broadcast_to(dl, (BQ, 128))

        @pl.when(jnp.logical_not(last))
        def _():
            scores(nxt, row1, pos1, n1 - 1, True)
            row_max()

        qT[...] = q[pl.ds(row0, BQ), :].T
        dT[...] = dom[pl.ds(row0, BQ), :].T
        dqa[...] = jnp.zeros((BQ, DH), f32)
        grads_in(slot, 0, 0)

        def pipe(c):
            grads_out(0, 2 * c)
            grads_in(slot, 1, 2 * c + 1)
            grads_out(1, 2 * c + 1)
            grads_in(slot, 0, 2 * c + 2)

        loop(0, n, pipe)
        dq[pl.ds(row0, BQ), :] = (dqa[...] * SCALE).astype(bf)

        @pl.when(j == NR - 1)
        def _():
            send_resp()

            @pl.when(side == 0)
            def _():
                send_other()

        @pl.when(j >= NR)
        def _():
            b = NP - 1 - (j - NR)
            pack_prompt(side * NT + b)
            for a in range(1, NT):

                @pl.when(lax.rem(t + a, NT) == b)
                def _():
                    prompt_copy(0, a).start()

    def two(i):
        block(2 * i, 0)
        block(2 * i + 1, 1)

    loop(0, NB // 2, two)

    @pl.when(side == 1)
    def _():
        send_other()

    def gather(rows, i, a):
        return [
            pltpu.make_async_remote_copy(
                src_ref=o.at[rows], dst_ref=o.at[rows],
                send_sem=g_s.at[2 * i + w, a], recv_sem=g_r.at[2 * i + w, a],
                device_id=peer(0, a), device_id_type=MESH,
            )
            for w, o in enumerate((dk, dv))
        ]

    rrows = pl.ds(pl.multiple_of(PH + t * SLR, SLR), SLR)
    prows = pl.ds(pl.multiple_of(t * SLP, SLP), SLP)
    total = sendR[t].astype(f32)
    for a in range(1, NT):
        resp_copy(a).wait_recv()
        total = total + recvR[a].astype(f32)
    dk[rrows, :] = total[:DH, :].T.astype(bf)
    dv[rrows, :] = total[DH:, :].T.astype(bf)
    for a in range(1, NT):
        for c in gather(rrows, 0, a):
            c.start()
    total = sendP[side * NT + t].astype(f32)
    for i in range(1, 2 * NT):
        prompt_copy(i // NT, i % NT).wait_recv()
        total = total + recvP[i].astype(f32)
    dk[prows, :] = total[:DH, :].T.astype(bf)
    dv[prows, :] = total[DH:, :].T.astype(bf)
    for a in range(1, NT):
        for c in gather(prows, 1, a):
            c.start()
    for c in kv:
        c.wait_send()
    for i in range(1, 2 * NT):
        prompt_copy(i // NT, i % NT).wait_send()
    for a in range(1, NT):
        resp_copy(a).wait_send()
        for c in gather(rrows, 0, a) + gather(prows, 1, a):
            c.wait()


def per_device(queries, keys, values, dout, offsets, lengths):
    V = pl.BlockSpec(memory_space=pltpu.VMEM)
    SM = pl.BlockSpec(memory_space=pltpu.SMEM)
    D = pltpu.SemaphoreType.DMA
    rows = PH + R
    big = pltpu.VMEM((BQ, KEYS + 256), f32)
    stat = pltpu.VMEM((BQ, 128), f32)
    return tuple(
        pl.pallas_call(
            kernel,
            out_shape=[jax.ShapeDtypeStruct((rows, DH), bf)] * 3,
            in_specs=[SM, SM, V, V, V, V],
            out_specs=[V, V, V],
            scratch_shapes=[
                pltpu.VMEM((KEYS, DH), bf), pltpu.VMEM((KEYS, DH), bf),
                pltpu.VMEM((DH, KEYS), f32), pltpu.VMEM((DH, KEYS), f32),
                big, big, big, big, big,
                *[pltpu.VMEM((BQ, 256), bf)] * 4,
                stat, stat, stat, stat,
                pltpu.VMEM((BQ, DH), f32), pltpu.VMEM((rows, DH), bf),
                pltpu.VMEM((DH, BQ), bf), pltpu.VMEM((DH, BQ), bf),
                pltpu.VMEM((8, KEYS), f32),
                pltpu.VMEM((2 * NT, 2 * DH, SLP), bf), pltpu.VMEM((NT, 2 * DH, SLR), bf),
                pltpu.VMEM((2 * NT, 2 * DH, SLP), bf), pltpu.VMEM((NT, 2 * DH, SLR), bf),
                D((4,)), D((4,)), D((2 * NT,)), D((2 * NT,)), D((NT,)), D((NT,)),
                D((4, NT)), D((4, NT)),
            ],
            compiler_params=pltpu.CompilerParams(
                collective_id=0, has_side_effects=True, vmem_limit_bytes=60 * 2**20
            ),
        )(offsets, lengths, queries, keys, values, dout)
    )


def solution(mesh):
    return jax.shard_map(
        per_device,
        mesh=mesh,
        in_specs=(P("dp", "tensor"), P("dp", None), P("dp", None), P("dp", "tensor"), P(), P("dp")),
        out_specs=(P("dp", "tensor"), P("dp", None), P("dp", None)),
        check_vma=False,
    )
```

time: 470 us -> 134 us (0.29)
  the two profiles are of different devices: /device:TPU:0 before, /device:TPU:2 now
where the time goes in v1:
time: 134 us
  Pallas kernels  129 us (96%)
  local copies, waits for them, and re-layouts  4.44 us (3%)
    pallas_call x1, Pallas kernels, per_device(): pl.pallas_call(kernel, out_shape=[jax.ShapeDtypeStruct((rows, DH), bf)] *...  129 us
    unnamed x7, local copies, waits for them, and re-layouts  4.44 us

profile of v1, /device:TPU:2, one launch (start us, length us, event | category | flops | bytes accessed | tf_op | source)
XLA Modules:
  0.0 134.2 jit_solution(2712947405015911726)
XLA Ops:
  1.3 128.5 %shard_map.85 = (bf16[3072,128]{1,0:T(8,128)(2,1)}, bf16[3072,128]{1,0:T(8,128)(2,1)}, bf16[3072,128]{1,0:T(8,128)(2,1)}) custom-call(s32[8]{0:T(128)} %offs.1, s32[1]{0:T(128)S(6)} %copy.12.lens, bf16[3072,128]{1,0:T(8,128)(2,1)} %q.1, bf16[3072,128]{1,0:T(8,128)(2,1)} %kin.1, bf16[3072,128]{1,0:T(8,128)(2,1)} %vin.1, bf16[3072,128]{1,0:T(8,128)(2,1)} %do.1), custom_call_target="tpu_custom_call" | custom-call | tf_op jit(solution)/shard_map/pallas_call | solution.py:324
  129.8 0.0 copy-start.1
  129.8 2.1 %copy.13 = bf16[3072,128]{1,0:T(8,128)(2,1)} copy(bf16[3072,128]{1,0:T(8,128)(2,1)} %get-tuple-element.6) | data formatting | bytes 1572864
  131.9 0.0 copy-done.1
  131.9 0.0 copy-start
  131.9 0.9 copy.14
  132.8 0.5 copy-done
  133.4 0.9 copy.15
Async XLA Ops:
  129.8 2.1 %copy-start.1 = (bf16[3072,128]{1,0:T(8,128)(2,1)S(1)}, bf16[3072,128]{1,0:T(8,128)(2,1)}, u32[]{:S(2)}) copy-start(bf16[3072,128]{1,0:T(8,128)(2,1)} %get-tuple-element.7) | copy-start | bytes 2359300
  131.9 1.4 %copy-start = (bf16[3072,128]{1,0:T(8,128)(2,1)S(1)}, bf16[3072,128]{1,0:T(8,128)(2,1)}, u32[]{:S(2)}) copy-start(bf16[3072,128]{1,0:T(8,128)(2,1)} %get-tuple-element.8) | copy-start | bytes 2359300
